TPU v7x, 256 devices: a whole 4x4x8 slice. The times are simulated.
256 devices in a mesh: cuts: 4 (over y_hi, core), fsdp: 64 (over y_lo, z, x).
Axes of the slice: x: 4, y: 4 (y_hi: 2, y_lo: 2; y = y_hi * 2 + y_lo), z: 8, core: 2. Of those that a mesh axis runs over, the one named last changes fastest.
Arguments:
- hidden_in: bfloat16 [65536, 8192], P(('cuts', 'fsdp')), may hold values from -24 to 24
- value_weight: bfloat16 [8192, 512], P('fsdp'), may hold values from -0.0625 to 0.0625
- queries: bfloat16 [65536, 4096], P(('cuts', 'fsdp')), may hold values from -100 to 100
- keys: bfloat16 [65536, 512], P(('cuts', 'fsdp')), may hold values from -5 to 5
- out_grad: bfloat16 [65536, 4096], P(('cuts', 'fsdp')), may hold values from -6 to 6
- new_logp: float32 [65536], P(('cuts', 'fsdp')), may hold values from -1.5 to -1
- old_logp: float32 [65536], P(('cuts', 'fsdp')), may hold values from -1.5 to -1
- rewards: float32 [256], P(('cuts', 'fsdp')), may hold values from -4 to 4
- resp_len: int32 [4, 64], P('cuts', 'fsdp'), may hold values from 1 to 256, 10240 in all within a row
- group_id: int32 [4, 64], P('cuts', 'fsdp'), may hold values from 0 to 7, never falling along the last dimension, each value on 1 to 16 neighbouring positions
Outputs:
- input_grad: bfloat16 [65536, 8192], P(('cuts', 'fsdp'))
- weight_grad: float32 [8192, 512], P('fsdp')
- clip_frac: float32 [], replicated
Inputs may be any that keep to these rules, and one draw needn't show every extreme that they name: `group_id`: group ids never fall along a slice's responses.
All inputs are finite; a program needn't handle non-finite values. No bound on the sum of `resp_len` on one device may be relied on, other than what follows from the above.
Results may differ from a plain program's by a relative error of at most 0.014.
Values may be sent and summed in bfloat16 or wider, within the bound.
A program may use at most 128 MiB of HBM per device.

v0:
```python
import jax
import jax.numpy as jnp
from jax import lax
from jax.sharding import PartitionSpec as P

HEAD = 128
KV_HEADS = 4
GROUP = 8


def value_grad(query_seq, key_seq, dout_seq):
    length = query_seq.shape[0]
    scale = 1.0 / HEAD**0.5
    rows = jnp.arange(length)
    allowed = rows[None, :] <= rows[:, None]
    query_heads = query_seq.reshape(length, KV_HEADS, GROUP, HEAD)
    key_heads = key_seq.reshape(length, KV_HEADS, HEAD)
    dout_heads = dout_seq.reshape(length, KV_HEADS, GROUP, HEAD)
    pieces = []
    for head in range(KV_HEADS):
        scores = (
            jnp.einsum(
                "igd,jd->gij",
                query_heads[:, head],
                key_heads[:, head],
                preferred_element_type=jnp.float32,
            )
            * scale
        )
        scores = jnp.where(allowed[None], scores, -1e30)
        top = jnp.max(scores, axis=2, keepdims=True)
        expo = jnp.exp(scores - top)
        probs = (expo / jnp.sum(expo, axis=2, keepdims=True)).astype(jnp.bfloat16)
        pieces.append(
            jnp.einsum(
                "gij,igd->jd", probs, dout_heads[:, head], preferred_element_type=jnp.float32
            )
        )
    return jnp.concatenate(pieces, axis=1).astype(jnp.bfloat16)


def local(
    hidden_in,
    value_weight,
    queries,
    keys,
    out_grad,
    new_logp,
    old_logp,
    rewards,
    resp_len,
    group_id,
):
    length = hidden_in.shape[0]
    n_cuts = lax.axis_size("cuts")
    n_fsdp = lax.axis_size("fsdp")
    n_groups = n_fsdp // 8
    live_len = resp_len.reshape(())
    own_group = group_id.reshape(())
    reward = rewards.reshape(())
    live = (jnp.arange(length) < live_len).astype(jnp.float32)
    ratio = jnp.exp(new_logp - old_logp)
    outside = jnp.logical_or(ratio > 1.28, ratio < 0.8).astype(jnp.float32)
    counts = jnp.stack([jnp.sum(live), jnp.sum(live * outside)])
    member = (jnp.arange(n_groups) == own_group).astype(jnp.float32)
    stats = jnp.stack([member, member * reward, member * (reward * reward)])
    group_totals = lax.psum(stats, "fsdp")
    totals = lax.psum(counts, ("cuts", "fsdp"))
    own_cnt = jnp.sum(group_totals[0] * member)
    own_one = jnp.sum(group_totals[1] * member)
    own_two = jnp.sum(group_totals[2] * member)
    mean = own_one / own_cnt
    var = own_two / own_cnt - mean * mean
    adv = (reward - mean) / jnp.sqrt(var + 0.25)
    total = totals[0]
    clip_frac = totals[1] / total
    active = jnp.where(adv > 0, ratio < 1.28, ratio > 0.8).astype(jnp.float32)
    coef = -live * adv * ratio * active * (length * n_cuts * n_fsdp / total)
    dout = (coef[:, None] * out_grad.astype(jnp.float32)).astype(jnp.bfloat16)
    dvalue = value_grad(queries, keys, dout)
    input_grad = lax.dot_general(
        dvalue,
        lax.all_gather(value_weight, "fsdp", axis=0, tiled=True),
        (((1,), (1,)), ((), ())),
        preferred_element_type=jnp.float32,
    ).astype(jnp.bfloat16)
    slice_part = lax.psum_scatter(
        lax.dot_general(
            hidden_in, dvalue, (((0,), (0,)), ((), ())), preferred_element_type=jnp.float32
        ),
        "fsdp",
        scatter_dimension=0,
        tiled=True,
    )
    weight_grad = lax.psum(slice_part.astype(jnp.bfloat16), "cuts").astype(jnp.float32)
    return (input_grad, weight_grad, clip_frac)


def solution(mesh):
    return jax.shard_map(
        local,
        mesh=mesh,
        in_specs=(
            P(("cuts", "fsdp"), None),
            P("fsdp", None),
            P(("cuts", "fsdp"), None),
            P(("cuts", "fsdp"), None),
            P(("cuts", "fsdp"), None),
            P(("cuts", "fsdp")),
            P(("cuts", "fsdp")),
            P(("cuts", "fsdp")),
            P("cuts", "fsdp"),
            P("cuts", "fsdp"),
        ),
        out_specs=(P(("cuts", "fsdp"), None), P("fsdp", None), P()),
        check_vma=False,
    )
```

profile of v0, /device:TPU:1, one launch (start us, length us, event | category | flops | bytes accessed | tf_op | source)
XLA Modules:
  0.0 995.9 jit_solution(9864744203813695453)
XLA Ops:
  7.2 0.0 reduce-scatter.2.cloned.1.call-start
  7.2 0.0 copy-start.2
  7.3 3.3 copy.21
  10.6 0.0 copy-done.2
  10.6 0.1 copy.19
  10.7 2.1 fusion.51
  12.9 2.1 fusion.50
  15.0 2.2 fusion.49
  17.1 0.0 copy-start.3
  17.1 0.0 copy-start.4
  17.1 2.1 fusion.48
  20.6 134.3 %psum.21 = f32[3,8]{1,0:T(4,128)S(1)} all-reduce(f32[3,8]{1,0:T(4,128)S(1)} %pad_maximum_fusion.3), channel_id=1, replica_groups=mesh['cuts'=4,'fsdp'=64] {'fsdp'}, use_global_device_ids=true, to_apply=%region_2.0 | all-reduce | flops 24 | bytes 192 | tf_op jit(solution)/shard_map/psum | solution.py:67
  154.9 0.7 fusion.31
  158.8 0.0 copy-done.3
  158.8 0.0 copy-done.4
  158.8 0.6 fusion.29
  159.5 1.3 pad_maximum_fusion.4
  160.8 101.2 %psum.22 = f32[2]{0:T(128)S(1)} all-reduce(f32[2]{0:T(128)S(1)} %pad_maximum_fusion.4), channel_id=1, replica_groups=mesh['cuts'=4,'fsdp'=64] {'cuts','fsdp'}, use_global_device_ids=true, to_apply=%region_8.9 | all-reduce | flops 2 | bytes 16 | tf_op jit(solution)/shard_map/psum | solution.py:68
  262.0 0.6 fusion.47
  263.2 2.2 multiply_convert_fusion
  265.4 2.5 copy.23
  267.8 0.0 copy-start.1
  267.9 0.0 copy-start.7
  267.9 2.3 fusion.8
  270.2 0.1 copy-done.1
  270.2 0.6 copy-done.7
  270.9 0.0 copy-start.6
  270.9 0.5 fusion.9
  271.4 1.1 copy-done.6
  272.5 0.0 copy-start.5
  272.5 0.5 fusion.10
  272.9 1.1 copy-done.5
  274.0 0.0 copy-start
  274.0 0.5 fusion.11
  274.5 1.7 copy-done
  276.2 8.1 convolution_bitcast_fusion
  284.3 0.0 reduce-scatter.2.cloned.1.call-update
  284.4 0.0 all-gather.2.cloned.1.call-start
  284.4 0.7 all-gather.2.cloned.1.call-update
  285.1 0.0 all-reduce.2.cloned.1.call-start
  286.4 299.8 %reduce-scatter.2.cloned.1.call-done = f32[128,512]{0,1:T(8,128)} async-done(((f32[8192,512]{0,1:T(8,128)}), f32[128,512]{0,1:T(8,128)}) %reduce-scatter.2.cloned.1.call-update) | async-done | bytes 262160 | tf_op jit(solution)/shard_map/reduce_scatter | solution.py:87
  586.3 1.6 convert_element_type.52
  587.9 0.0 all-reduce.2.cloned.1.call-update
  587.9 311.3 %all-gather.2.cloned.1.call-done = bf16[8192,512]{1,0:T(8,128)(2,1)} async-done(((bf16[128,512]{1,0:T(8,128)(2,1)}), bf16[8192,512]{1,0:T(8,128)(2,1)}) %all-gather.2.cloned.1.call-update) | async-done | bytes 8388624 | tf_op jit(solution)/shard_map/all_gather | solution.py:83
  899.2 7.8 convolution_convert_fusion
  907.0 79.5 %all-reduce.2.cloned.1.call-done = bf16[128,512]{0,1:T(8,128)(2,1)} async-done(((bf16[128,512]{0,1:T(8,128)(2,1)}), bf16[128,512]{0,1:T(8,128)(2,1)}) %all-reduce.2.cloned.1.call-update) | async-done | bytes 131088 | tf_op jit(solution)/shard_map/psum | solution.py:95
  986.5 1.7 copy.34
  (5 shorter events, 0.1 us)
Async XLA Ops:
  7.2 579.1 %reduce-scatter.2.cloned.1.call-start = ((), (), s32[]{:S(2)}) async-start(), calls=%async_computation.2 | async-start | bytes 17039360 | tf_op jit(solution)/shard_map/reduce_scatter | solution.py:87
  7.2 3.3 copy-start.2
  17.1 141.7 %copy-start.3 = (f32[256]{0:T(256)S(1)}, f32[256]{0:T(256)}, u32[]{:S(2)}) copy-start(f32[256]{0:T(256)} %param.15) | copy-start | bytes 3076
  17.1 141.7 %copy-start.4 = (f32[256]{0:T(256)S(1)}, f32[256]{0:T(256)}, u32[]{:S(2)}) copy-start(f32[256]{0:T(256)} %param.16) | copy-start | bytes 3076
  267.8 2.4 copy-start.1
  267.9 3.0 copy-start.7
  270.9 1.6 copy-start.6
  272.5 1.6 copy-start.5
  274.0 2.2 copy-start
  284.4 614.8 %all-gather.2.cloned.1.call-start = ((), (), s32[]{:S(2)}) async-start(), calls=%async_computation.1 | async-start | bytes 8519680 | tf_op jit(solution)/shard_map/all_gather | solution.py:83
  285.1 701.4 %all-reduce.2.cloned.1.call-start = ((), (), s32[]{:S(2)}) async-start(), calls=%async_computation.3 | async-start | bytes 262144 | tf_op jit(solution)/shard_map/psum | solution.py:95
Sparse Core Ops, SparseCore 0:
  284.5 301.7 reduce-scatter.1
  588.0 311.1 all-gather.1
  902.4 84.0 all-reduce.1
where the time goes:
time: 996 us
  waiting for transfers between devices  691 us (69%)
  blocking collectives  235 us (24%)
  matrix products  28.2 us (3%)
  between operations  21.4 us (2%)
  local copies, waits for them, and re-layouts  12.8 us (1%)
    all_gather x1, waiting for transfers between devices, local(): lax.all_gather(value_weight, 'fsdp', axis=0, tiled=True)  311 us
    reduce_scatter x1, waiting for transfers between devices, local(): lax.psum_scatter(lax.dot_general(hidden_in, dvalue, (((0,), (0,)), ((), (...  300 us
    psum x1, blocking collectives, local(): group_totals = lax.psum(stats, 'fsdp')  134 us
    psum x1, blocking collectives, local(): totals = lax.psum(counts, ('cuts', 'fsdp'))  101 us
    psum x1, waiting for transfers between devices, local(): lax.psum(slice_part.astype(jnp.bfloat16), 'cuts').astype(jnp.float32)  79.5 us
  transfers between devices with their start and end apart: 3, of which 3 were waited for; matrix products, arithmetic and copies ran while one was open for 1% of the time, Pallas kernels for 0%

commit v1 on v0

v1 whole, which is shorter than its diff:
```python
import functools

import jax
import jax.numpy as jnp
from jax import lax
from jax.experimental import pallas as pl
from jax.experimental.pallas import tpu as pltpu
from jax.sharding import PartitionSpec as P

HEAD = 128
KV_HEADS = 4
GROUP = 8
LEN = 256
D = 8192
F32 = jnp.float32
BF16 = jnp.bfloat16
MESH = pl.DeviceIdType.MESH
N_X, N_Y, N_Z = 4, 4, 8
RA, RB, RC = 48, 32, 48
SLOTS = 192


def _coords():
    cuts = lax.axis_index("cuts")
    fsdp = lax.axis_index("fsdp")
    core = cuts % 2
    y_hi = cuts // 2
    y_lo = fsdp // 32
    z = (fsdp // 4) % 8
    x = fsdp % 4
    return x, y_hi * 2 + y_lo, z, core


def _device(x, y, z, core):
    return ((y // 2) * 2 + core, (y % 2) * 32 + z * 4 + x)


def _nt(a, b):
    return lax.dot_general(a, b, (((1,), (1,)), ((), ())), preferred_element_type=F32)


def _nn(a, b):
    return lax.dot_general(a, b, (((1,), (0,)), ((), ())), preferred_element_type=F32)


def kernel(
    hid, w, q, k, og, nlp, olp, rew, rlen, gid,
    ig, wg, cf,
    hv, qv, ogv, pt, douts, dvs, dvr, dvt, W, out,
    PA, PB, PC, rax, ray, raz, rcy, rcx, rcz, rbz, rbx, rby,
    fin, st, rsz, rsx, rsy, rsc, coefv,
    ssem, rsem, lsem, osem,
):
    x, y, z, c = _coords()
    y_lo, y_hi = y % 2, y // 2

    def xs(d):
        return (x + d + N_X) % N_X

    def ys(d):
        return (y + d + N_Y) % N_Y

    def zs(d):
        return (z + d + N_Z) % N_Z

    def at_x(d):
        return _device(xs(d), y, z, c)

    def at_y(d):
        return _device(x, ys(d), z, c)

    def at_z(d):
        return _device(x, y, zs(d), c)

    partner = _device(x, y, z, 1 - c)
    sent = []

    def send(src, dst, device):
        i = len(sent)
        copy = pltpu.make_async_remote_copy(
            src_ref=src, dst_ref=dst, send_sem=ssem.at[i], recv_sem=rsem.at[i],
            device_id=device, device_id_type=MESH,
        )
        copy.start()
        sent.append(copy)
        return copy

    loads = [
        pltpu.make_async_copy(q, qv, lsem.at[0]),
        pltpu.make_async_copy(og, ogv, lsem.at[1]),
        pltpu.make_async_copy(hid, hv.at[0], lsem.at[2]),
    ]
    for load in loads:
        load.start()

    barrier = pltpu.get_barrier_semaphore()
    around = [at_x(1), at_x(-1), at_x(2), at_y(1), at_y(-1), at_y(2), partner]
    around += [at_z(d) for d in range(1, 8)]
    around += [_device(x, ys(2), z, 1 - c)]
    for device in around:
        pl.semaphore_signal(barrier, inc=1, device_id=device, device_id_type=MESH)

    W[c, y_lo, z, x] = w[pl.ds(pl.multiple_of(64 * c, 64), 64), :]
    lane = lax.broadcasted_iota(jnp.int32, (8, 128), 1)
    group = gid[...]
    reward = rew[...]
    length = rlen[...].astype(F32)
    position = lax.broadcasted_iota(jnp.int32, (1, LEN), 1)
    live = (position < rlen[...]).astype(F32)
    ratio = jnp.exp(nlp[...] - olp[...])
    outside = jnp.logical_or(ratio > 1.28, ratio < 0.8).astype(F32)
    clipped = jnp.sum(live * outside, axis=1, keepdims=True)
    member = (lane % 8 == group).astype(F32)
    stats = jnp.where(
        lane < 8, member,
        jnp.where(
            lane < 16, member * reward,
            jnp.where(
                lane < 24, member * (reward * reward),
                jnp.where(lane == 24, length, jnp.where(lane == 25, clipped, 0.0)),
            ),
        ),
    )
    st[0] = stats
    pl.semaphore_wait(barrier, len(around))

    def stats_steps():
        copies = [send(st.at[0], rsz.at[d - 1], at_z(d)) for d in range(1, 8)]
        yield
        for copy in copies:
            copy.wait_recv()
        total = st[0]
        for i in range(7):
            total = total + rsz[i]
        st[1] = total
        copies = [send(st.at[1], rsx.at[d - 1], at_x(d)) for d in range(1, 4)]
        yield
        for copy in copies:
            copy.wait_recv()
        st[2] = (st[1] + rsx[0]) + (rsx[1] + rsx[2])
        other = _device(x, y_hi * 2 + (1 - y_lo), z, c)
        copy = send(st.at[2], rsy, other)
        yield
        copy.wait_recv()
        st[3] = st[2] + rsy[...]
        copies = [
            send(st.at[3], rsc.at[0], at_y(2)),
            send(st.at[3], rsc.at[1], partner),
            send(st.at[3], rsc.at[2], _device(x, ys(2), z, 1 - c)),
        ]
        yield
        for copy in copies:
            copy.wait_recv()
        every = ((st[3] + rsc[0]) + (rsc[1] + rsc[2]))[0:1]
        top = lane[0:1]
        all_live = jnp.sum(jnp.where(top == 24, every, 0.0), axis=1, keepdims=True)
        all_out = jnp.sum(jnp.where(top == 25, every, 0.0), axis=1, keepdims=True)
        cf[...] = all_out / all_live

    def ring_z(view, half):
        up = send(view(z), view(z), at_z(1))
        down = send(view(z), view(z), at_z(-1))
        yield
        for d in (1, 2, 3):
            up.wait_recv()
            down.wait_recv()
            if d < 3:
                up = send(view(zs(-d)), view(zs(-d)), at_z(1))
                down = send(view(zs(d)), view(zs(d)), at_z(-1))
            else:
                up = send(half(zs(-3), 0), half(zs(-3), 0), at_z(1))
                down = send(half(zs(3), 1), half(zs(3), 1), at_z(-1))
            yield
        up.wait_recv()
        down.wait_recv()

    forwards = []

    def gather_a():
        own = W.at[c, y_lo, z, x, pl.ds(0, 16)]
        copy = send(own, own, at_y(1))
        yield
        copy.wait_recv()
        yield from ring_z(
            lambda i: W.at[c, :, i, x, pl.ds(0, 16)],
            lambda i, h: W.at[c, h, i, x, pl.ds(0, 16)],
        )

        def view(i):
            return W.at[c, :, :, i, pl.ds(0, 16)]

        def half(i, h):
            return W.at[c, h, :, i, pl.ds(0, 16)]

        up = send(view(x), view(x), at_x(1))
        down = send(view(x), view(x), at_x(-1))
        forwards.append(send(view(x), view(x), partner))
        yield
        up.wait_recv()
        down.wait_recv()
        up = send(half(xs(-1), 0), half(xs(-1), 0), at_x(1))
        down = send(half(xs(1), 1), half(xs(1), 1), at_x(-1))
        forwards.append(send(view(xs(-1)), view(xs(-1)), partner))
        forwards.append(send(view(xs(1)), view(xs(1)), partner))
        yield
        up.wait_recv()
        down.wait_recv()
        forwards.append(send(view(xs(2)), view(xs(2)), partner))

    def gather_b():
        own = W.at[c, y_lo, z, x, pl.ds(16, 16)]
        copies = [send(own, own, at_x(d)) for d in (1, 2, 3)]
        yield
        for copy in copies:
            copy.wait_recv()
        left = W.at[c, y_lo, z, pl.ds(0, 2), pl.ds(16, 16)]
        right = W.at[c, y_lo, z, pl.ds(2, 2), pl.ds(16, 16)]
        copies = [send(left, left, at_y(1)), send(right, right, at_y(-1))]
        yield
        for copy in copies:
            copy.wait_recv()
        def view(i):
            return W.at[c, :, i, :, pl.ds(16, 16)]

        yield from ring_z(view, lambda i, h: W.at[c, h, i, :, pl.ds(16, 16)])
        whole = W.at[c, :, :, :, pl.ds(16, 16)]
        forwards.append(send(whole, whole, partner))

    def gather_c():
        yield from ring_z(
            lambda i: W.at[c, y_lo, i, x, pl.ds(32, 32)],
            lambda i, h: W.at[c, y_lo, i, x, pl.ds(32 + 16 * h, 16)],
        )
        final = []

        def view(i):
            return W.at[c, y_lo, :, i, pl.ds(32, 32)]

        def half(i, h):
            return W.at[c, y_lo, pl.ds(4 * h, 4), i, pl.ds(32, 32)]

        def across(i):
            final.append(send(half(i, 0), half(i, 0), at_y(1)))
            final.append(send(half(i, 1), half(i, 1), at_y(-1)))

        up = send(view(x), view(x), at_x(1))
        down = send(view(x), view(x), at_x(-1))
        across(x)
        yield
        up.wait_recv()
        down.wait_recv()
        up = send(half(xs(-1), 0), half(xs(-1), 0), at_x(1))
        down = send(half(xs(1), 1), half(xs(1), 1), at_x(-1))
        across(xs(-1))
        across(xs(1))
        yield
        up.wait_recv()
        down.wait_recv()
        across(xs(2))
        mine = W.at[c, y_lo, :, :, pl.ds(32, 32)]
        forwards.append(send(mine, mine, partner))
        yield
        for copy in final:
            copy.wait_recv()
        theirs = W.at[c, 1 - y_lo, :, :, pl.ds(32, 32)]
        forwards.append(send(theirs, theirs, partner))

    def advance(steps):
        for step in list(steps):
            if next(step, "end") == "end":
                steps.remove(step)

    stat = [stats_steps()]
    gather = [gather_a(), gather_b(), gather_c()]
    advance(stat)
    advance(gather)
    hidden_copy = send(hid, hv.at[1], partner)

    loads[0].wait()
    factor = (1.0 / HEAD**0.5) * 1.4426950408889634
    row = lax.broadcasted_iota(jnp.int32, (HEAD, HEAD), 0)
    col = lax.broadcasted_iota(jnp.int32, (HEAD, HEAD), 1)
    causal = row <= col

    def soft(scores):
        top = jnp.max(scores, axis=0, keepdims=True)
        expo = jnp.exp2((scores - top) * factor)
        return (expo * (1.0 / jnp.sum(expo, axis=0, keepdims=True))).astype(BF16)

    def attend(head, first):
        keys = k[:, head * HEAD:(head + 1) * HEAD]

        def one(i, carry):
            g = first + i
            n = head * GROUP + g
            query = qv[:, pl.ds(pl.multiple_of(n * HEAD, HEAD), HEAD)]
            early = jnp.where(causal, _nt(keys[:128], query[:128]), -1e30)
            late = _nt(keys, query[128:])
            late = jnp.concatenate([late[:128], jnp.where(causal, late[128:], -1e30)], axis=0)
            at = pl.multiple_of(g * LEN, LEN)
            pt[head, pl.ds(0, 128), pl.ds(at, 128)] = soft(early)
            pt[head, pl.ds(128, 128), pl.ds(at, 128)] = jnp.zeros((128, 128), BF16)
            pt[head, :, pl.ds(at + 128, 128)] = soft(late)
            return carry

        lax.fori_loop(0, 4, one, 0)

    for part in range(8):
        attend(part // 2, 4 * (part % 2))
        advance(stat)
        advance(gather)

    slice_total = st[3][0:1]
    top = lane[0:1]

    def pick(at):
        return jnp.sum(jnp.where(top == at, slice_total, 0.0), axis=1, keepdims=True)

    own_cnt, own_one, own_two = pick(group), pick(8 + group), pick(16 + group)
    mean = own_one / own_cnt
    var = own_two / own_cnt - mean * mean
    adv = (reward - mean) / jnp.sqrt(var + 0.25)
    total = pick(24) * 4.0
    active = jnp.where(adv > 0, (ratio < 1.28).astype(F32), (ratio > 0.8).astype(F32))
    coef = -live * adv * ratio * active * (65536.0 / total)
    diagonal = lax.broadcasted_iota(jnp.int32, (LEN, LEN), 0) == lax.broadcasted_iota(jnp.int32, (LEN, LEN), 1)
    coefv[...] = jnp.broadcast_to(
        jnp.sum(jnp.where(diagonal, coef, 0.0), axis=1, keepdims=True), (LEN, HEAD)
    )
    loads[1].wait()
    for head in range(KV_HEADS):
        for g in range(GROUP):
            n = head * GROUP + g
            douts[g * LEN:(g + 1) * LEN, :] = (
                coefv[...] * ogv[:, n * HEAD:(n + 1) * HEAD].astype(F32)
            ).astype(BF16)
        dvs[head // 2, :, (head % 2) * HEAD:(head % 2 + 1) * HEAD] = _nn(pt[head], douts[...]).astype(BF16)
    dv_copy = send(dvs.at[1 - c], dvr, partner)
    advance(gather)
    loads[2].wait()
    hidden_copy.wait_recv()
    dvt[:, 0:LEN] = dvs[c].T
    dv_copy.wait_recv()
    dvt[:, LEN:2 * LEN] = dvr[...].T

    def partial(t, carry):
        yl, zz = t // 8, t % 8
        columns = pl.ds(pl.multiple_of(t * 512, 512), 512)
        block = _nn(dvt[:, 0:LEN], hv[0, :, columns]) + _nn(dvt[:, LEN:2 * LEN], hv[1, :, columns])
        block = block.astype(BF16)
        for i in range(N_X):
            b = block[:, i * 128:(i + 1) * 128]
            PA[yl, zz, i, 0] = b[0:48]
            PA[yl, zz, i, 1] = b[48:96]
            PB[yl, zz, i, 0] = b[96:128]
            PB[yl, zz, i, 1] = b[128:160]
            PC[yl, zz, i, 0] = b[160:208]
            PC[yl, zz, i, 1] = b[208:256]
        return carry

    lax.fori_loop(0, 16, partial, 0)

    def added(*terms):
        total = terms[0].astype(F32)
        for term in terms[1:]:
            total = total + term.astype(F32)
        return total

    def reduce_a():
        up = send(PA.at[:, :, xs(2), 0], rax.at[0], at_x(1))
        down = send(PA.at[:, :, xs(2), 1], rax.at[1], at_x(-1))
        up_b = send(PA.at[:, :, xs(1), 1], rax.at[2], at_x(1))
        down_b = send(PA.at[:, :, xs(-1), 0], rax.at[3], at_x(-1))
        yield
        up.wait_recv()
        PA[:, :, xs(1), 0] = added(PA[:, :, xs(1), 0], rax[0]).astype(BF16)
        up = send(PA.at[:, :, xs(1), 0], rax.at[4], at_x(1))
        down.wait_recv()
        PA[:, :, xs(-1), 1] = added(PA[:, :, xs(-1), 1], rax[1]).astype(BF16)
        down = send(PA.at[:, :, xs(-1), 1], rax.at[5], at_x(-1))
        yield
        up_b.wait_recv()
        down_b.wait_recv()
        up.wait_recv()
        down.wait_recv()
        PA[:, :, x, 0] = added(PA[:, :, x, 0], rax[3], rax[4]).astype(BF16)
        PA[:, :, x, 1] = added(PA[:, :, x, 1], rax[2], rax[5]).astype(BF16)
        copies = [send(PA.at[ys(d) % 2, :, x, ys(d) // 2], ray.at[d - 1], at_y(d)) for d in (2, 1, 3)]
        yield
        for copy in copies:
            copy.wait_recv()
        PA[y_lo, :, x, y_hi] = added(PA[y_lo, :, x, y_hi], ray[0], ray[1], ray[2]).astype(BF16)
        copies = [send(PA.at[y_lo, zs(d), x, y_hi], raz.at[d - 1], at_z(d)) for d in (4, 3, 5, 2, 6, 1, 7)]
        yield
        for copy in copies:
            copy.wait_recv()
        fin[y_hi, c, pl.ds(0, RA)] = added(PA[y_lo, z, x, y_hi], *[raz[i] for i in range(7)]).astype(BF16)

    def reduce_c():
        def view(d, h):
            return PC.at[ys(d) % 2, pl.ds(4 * h, 4), :, ys(d) // 2]

        def get(d, h):
            return PC[ys(d) % 2, pl.ds(4 * h, 4), :, ys(d) // 2]

        def put(d, h, value):
            PC[ys(d) % 2, pl.ds(4 * h, 4), :, ys(d) // 2] = value.astype(BF16)

        up = send(view(2, 0), rcy.at[0], at_y(1))
        down = send(view(2, 1), rcy.at[1], at_y(-1))
        up_b = send(view(1, 1), rcy.at[2], at_y(1))
        down_b = send(view(-1, 0), rcy.at[3], at_y(-1))
        yield
        up.wait_recv()
        put(1, 0, added(get(1, 0), rcy[0]))
        up = send(view(1, 0), rcy.at[4], at_y(1))
        down.wait_recv()
        put(-1, 1, added(get(-1, 1), rcy[1]))
        down = send(view(-1, 1), rcy.at[5], at_y(-1))
        yield
        up_b.wait_recv()
        down_b.wait_recv()
        up.wait_recv()
        down.wait_recv()
        put(0, 0, added(get(0, 0), rcy[3], rcy[4]))
        put(0, 1, added(get(0, 1), rcy[2], rcy[5]))
        copies = [send(PC.at[y_lo, :, xs(d), y_hi], rcx.at[d - 1], at_x(d)) for d in (2, 1, 3)]
        yield
        for copy in copies:
            copy.wait_recv()
        PC[y_lo, :, x, y_hi] = added(PC[y_lo, :, x, y_hi], rcx[0], rcx[1], rcx[2]).astype(BF16)
        copies = [send(PC.at[y_lo, zs(d), x, y_hi], rcz.at[d - 1], at_z(d)) for d in (4, 3, 5, 2, 6, 1, 7)]
        yield
        for copy in copies:
            copy.wait_recv()
        fin[y_hi, c, pl.ds(RA + RB, RC)] = added(
            PC[y_lo, z, x, y_hi], *[rcz[i] for i in range(7)]
        ).astype(BF16)

    def reduce_b():
        up = send(PB.at[:, zs(4), :, 0], rbz.at[0, :, :, 0], at_z(1))
        down = send(PB.at[:, zs(4), :, 1], rbz.at[0, :, :, 1], at_z(-1))
        yield
        up.wait_recv()
        PB[:, zs(3), :, 0] = added(PB[:, zs(3), :, 0], rbz[0, :, :, 0]).astype(BF16)
        up = send(PB.at[:, zs(3)], rbz.at[1], at_z(1))
        down.wait_recv()
        PB[:, zs(-3), :, 1] = added(PB[:, zs(-3), :, 1], rbz[0, :, :, 1]).astype(BF16)
        down = send(PB.at[:, zs(-3)], rbz.at[2], at_z(-1))
        yield
        for d in (2, 1):
            up.wait_recv()
            PB[:, zs(d)] = added(PB[:, zs(d)], rbz[5 - 2 * d]).astype(BF16)
            up = send(PB.at[:, zs(d)], rbz.at[7 - 2 * d], at_z(1))
            down.wait_recv()
            PB[:, zs(-d)] = added(PB[:, zs(-d)], rbz[6 - 2 * d]).astype(BF16)
            down = send(PB.at[:, zs(-d)], rbz.at[8 - 2 * d], at_z(-1))
            yield
        up.wait_recv()
        down.wait_recv()
        PB[:, z] = added(PB[:, z], rbz[5], rbz[6]).astype(BF16)
        copies = [send(PB.at[:, z, xs(d)], rbx.at[d - 1], at_x(d)) for d in (2, 1, 3)]
        yield
        for copy in copies:
            copy.wait_recv()
        PB[:, z, x] = added(PB[:, z, x], rbx[0], rbx[1], rbx[2]).astype(BF16)
        copies = [send(PB.at[ys(d) % 2, z, x, ys(d) // 2], rby.at[d - 1], at_y(d)) for d in (2, 1, 3)]
        yield
        for copy in copies:
            copy.wait_recv()
        fin[y_hi, c, pl.ds(RA, RB)] = added(PB[y_lo, z, x, y_hi], rby[0], rby[1], rby[2]).astype(BF16)

    scatter = [reduce_a(), reduce_c(), reduce_b()]
    advance(scatter)
    while gather:
        advance(gather)
        advance(scatter)
    for copy in forwards:
        copy.wait_recv()

    dv = jnp.concatenate([dvs[0], dvs[1]], axis=1)

    def stored(t):
        columns = pl.ds(pl.multiple_of(t * 512, 512), 512)
        return pltpu.make_async_copy(out.at[:, columns], ig.at[:, columns], osem.at[t])

    def product(t, carry):
        yl, zz = t // 8, t % 8
        rows = jnp.concatenate([W[h, yl, zz, i] for i in range(N_X) for h in range(2)], axis=0)
        out[:, pl.ds(pl.multiple_of(t * 512, 512), 512)] = _nt(dv, rows).astype(BF16)
        stored(t).start()
        return carry

    lax.fori_loop(0, 16, product, 0)

    while scatter:
        advance(scatter)
    mine = fin.at[y_hi, c]
    copies = [
        send(mine, mine, at_y(2)),
        send(mine, mine, partner),
        send(mine, mine, _device(x, ys(2), z, 1 - c)),
    ]
    for copy in copies:
        copy.wait_recv()
    pieces = []
    for core in range(2):
        for first, size in ((0, RA), (RA, RB), (RA + RB, RC)):
            for half in range(2):
                pieces.append(fin[half, core, pl.ds(first, size)])
    wg[...] = jnp.concatenate(pieces, axis=0).astype(F32).T

    while stat:
        advance(stat)

    def waited(t, carry):
        stored(t).wait()
        return carry

    lax.fori_loop(0, 16, waited, 0)
    for copy in sent:
        copy.wait_send()


def local(
    hidden_in, value_weight, queries, keys, out_grad, new_logp, old_logp, rewards, resp_len, group_id
):
    vmem = pl.BlockSpec(memory_space=pltpu.VMEM)
    hbm = pl.BlockSpec(memory_space=pl.ANY)
    bf = functools.partial(pltpu.VMEM, dtype=BF16)
    scratch = [
        bf((2, LEN, D)),
        bf((LEN, 4096)),
        bf((LEN, 4096)),
        bf((KV_HEADS, LEN, GROUP * LEN)),
        bf((GROUP * LEN, HEAD)),
        bf((2, LEN, 256)),
        bf((LEN, 256)),
        bf((256, 2 * LEN)),
        bf((2, 2, 8, 4, 64, 512)),
        bf((LEN, D)),
        bf((2, 8, 4, 2, RA, 128)),
        bf((2, 8, 4, 2, RB, 128)),
        bf((2, 8, 4, 2, RC, 128)),
        bf((6, 2, 8, RA, 128)),
        bf((3, 8, RA, 128)),
        bf((7, RA, 128)),
        bf((6, 4, 4, RC, 128)),
        bf((3, 8, RC, 128)),
        bf((7, RC, 128)),
        bf((7, 2, 4, 2, RB, 128)),
        bf((3, 2, 2, RB, 128)),
        bf((3, RB, 128)),
        bf((2, 2, 128, 128)),
        pltpu.VMEM((4, 8, 128), F32),
        pltpu.VMEM((7, 8, 128), F32),
        pltpu.VMEM((3, 8, 128), F32),
        pltpu.VMEM((8, 128), F32),
        pltpu.VMEM((3, 8, 128), F32),
        pltpu.VMEM((LEN, HEAD), F32),
        pltpu.SemaphoreType.DMA((SLOTS,)),
        pltpu.SemaphoreType.DMA((SLOTS,)),
        pltpu.SemaphoreType.DMA((3,)),
        pltpu.SemaphoreType.DMA((16,)),
    ]
    input_grad, weight_grad, clip_frac = pl.pallas_call(
        kernel,
        out_shape=(
            jax.ShapeDtypeStruct((LEN, D), BF16),
            jax.ShapeDtypeStruct((128, 512), F32),
            jax.ShapeDtypeStruct((1, 1), F32),
        ),
        in_specs=[hbm, vmem, hbm, vmem, hbm, vmem, vmem, vmem, vmem, vmem],
        out_specs=(hbm, vmem, vmem),
        scratch_shapes=scratch,
        compiler_params=pltpu.CompilerParams(
            collective_id=0, has_side_effects=True, vmem_limit_bytes=56 << 20
        ),
        name="value_backward",
    )(
        hidden_in, value_weight, queries, keys, out_grad,
        new_logp.reshape(1, LEN), old_logp.reshape(1, LEN), rewards.reshape(1, 1), resp_len, group_id,
    )
    return input_grad, weight_grad, clip_frac.reshape(())


def solution(mesh):
    rows = P(("cuts", "fsdp"), None)
    flat = P(("cuts", "fsdp"))
    return jax.shard_map(
        local,
        mesh=mesh,
        in_specs=(
            rows, P("fsdp", None), rows, rows, rows, flat, flat, flat, P("cuts", "fsdp"), P("cuts", "fsdp"),
        ),
        out_specs=(rows, P("fsdp", None), P()),
        check_vma=False,
    )
```

time: 996 us -> 115 us (0.12)
  waiting for transfers between devices: 691 us -> 0 us
  blocking collectives: 235 us -> 0 us
  Pallas kernels: 0 us -> 105 us
  matrix products: 28.2 us -> 0 us
  between operations: 21.4 us -> 4.35 us
    all_gather x1 -> x0, waiting for transfers between devices: 311 us -> none  [local(): lax.all_gather(value_weight, 'fsdp', axis=0, tiled=True)]
    reduce_scatter x1 -> x0, waiting for transfers between devices: 300 us -> none  [local(): lax.psum_scatter(lax.dot_general(hidden_in, dvalue, (((0,), (0,)), ((), (...]
    psum x2 -> x0, blocking collectives: 235 us -> none  [the longest x1 134 us: local(): group_totals = lax.psum(stats, 'fsdp')]
    pallas_call x0 -> x1, Pallas kernels: none -> 105 us  [local(): pl.pallas_call(kernel, out_shape=(jax.ShapeDtypeStruct((LEN, D), BF16), j...]
    psum x1 -> x0, waiting for transfers between devices: 79.5 us -> none  [local(): lax.psum(slice_part.astype(jnp.bfloat16), 'cuts').astype(jnp.float32)]
    dot_general x6 -> x0, matrix products: 19.7 us -> none  [the longest x1 8.1 us: local(): lax.dot_general(hidden_in, dvalue, (((0,), (0,)), ((), ())), preferred_el...]
  transfers between devices with their start and end apart: 3 -> 0, of which waited for: 3 -> 0; matrix products, arithmetic and copies ran while one was open for 1% -> 0% of each run, Pallas kernels for 0% -> 0%
where the time goes in v1:
time: 115 us
  Pallas kernels  105 us (91%)
  local copies, waits for them, and re-layouts  5.39 us (5%)
  between operations  4.35 us (4%)
    pallas_call x1, Pallas kernels, local(): pl.pallas_call(kernel, out_shape=(jax.ShapeDtypeStruct((LEN, D), BF16), j...  105 us
    unnamed x4, local copies, waits for them, and re-layouts  5.39 us

profile of v1, /device:TPU:1, one launch (start us, length us, event | category | flops | bytes accessed | tf_op | source)
XLA Modules:
  0.0 114.6 jit_solution(17445929407046096029)
XLA Ops:
  2.6 104.9 %value_backward.1 = (bf16[256,8192]{1,0:T(8,128)(2,1)}, f32[128,512]{1,0:T(8,128)}, f32[1,1]{1,0:T(1,128)}) custom-call(bf16[256,8192]{1,0:T(8,128)(2,1)} %hid.1, bf16[128,512]{1,0:T(8,128)(2,1)} %w.1, bf16[256,4096]{1,0:T(8,128)(2,1)} %q.1, bf16[256,512]{1,0:T(8,128)(2,1)} %k.1, bf16[256,4096]{1,0:T(8,128)(2,1)} %og.1, f32[1,256]{1,0:T(1,128)} %bitcast.5, ...), custom_call_target="tpu_custom_call" | custom-call | tf_op jit(solution)/shard_map/value_backward/pallas_call | solution.py:566
  107.5 0.0 copy-start
  107.5 4.7 %copy.19 = bf16[256,8192]{1,0:T(8,128)(2,1)} copy(bf16[256,8192]{1,0:T(8,128)(2,1)} %get-tuple-element.12) | data formatting | bytes 8388608
  112.1 0.0 copy-done
  112.1 0.7 copy.20
Async XLA Ops:
  107.5 4.7 %copy-start = (f32[128,512]{1,0:T(8,128)S(1)}, f32[128,512]{1,0:T(8,128)}, u32[]{:S(2)}) copy-start(f32[128,512]{1,0:T(8,128)} %get-tuple-element.13) | copy-start | bytes 786436

commit v2 on v1

v2 whole, which is shorter than its diff:
```python
import functools

import jax
import jax.numpy as jnp
from jax import lax
from jax.experimental import pallas as pl
from jax.experimental.pallas import tpu as pltpu
from jax.sharding import PartitionSpec as P

HEAD = 128
KV_HEADS = 4
GROUP = 8
LEN = 256
D = 8192
F32 = jnp.float32
BF16 = jnp.bfloat16
MESH = pl.DeviceIdType.MESH
N_X, N_Y, N_Z = 4, 4, 8
RA, RB, RC = 32, 32, 64
SLOTS = 192
ORDER = (
    "stat", "ga", "gb", "gc", "att", "att", "att", "att", "ga", "att",
    "att", "gb", "att", "stat", "gc", "att", "gb", "ga", "gc", "stat",
    "coef", "pass2a", "pass2b", "part0", "rb", "gb", "part1", "rc", "ga", "part2",
    "part3", "ra", "gc", "rc", "rb", "rd", "rd", "gb", "rc", "rb",
    "ga", "gb", "ra", "rb", "gb", "rd", "gc", "gb", "rb", "ga",
    "ga", "rc", "ra", "rb", "rd", "rc", "gc", "rd", "ra", "gc",
    "prod", "rb", "rc", "prod", "prod", "prod", "prod", "rd", "prod", "prod",
    "ra", "prod",
)


def _coords():
    cuts = lax.axis_index("cuts")
    fsdp = lax.axis_index("fsdp")
    core = cuts % 2
    y_hi = cuts // 2
    y_lo = fsdp // 32
    z = (fsdp // 4) % 8
    x = fsdp % 4
    return x, y_hi * 2 + y_lo, z, core


def _device(x, y, z, core):
    return ((y // 2) * 2 + core, (y % 2) * 32 + z * 4 + x)


def _nt(a, b):
    return lax.dot_general(a, b, (((1,), (1,)), ((), ())), preferred_element_type=F32)


def _nn(a, b):
    return lax.dot_general(a, b, (((1,), (0,)), ((), ())), preferred_element_type=F32)


def kernel(
    hid, w, q, k, og, nlp, olp, rew, rlen, gid,
    ig, wg, cf,
    hv, qv, ogv, kv, pt, douts, dvs, dvf, dvr, dvt, W,
    PA, PB, PC, rax, ray, raz, rcy, rcx, rcz, rbz, rbx, rby,
    fin, st, rsp, rsz, rsc, coefv,
    ssem, rsem, lsem, nlv, olv, rwv, rlv, giv,
):
    x, y, z, c = _coords()
    y_lo, y_hi = y % 2, y // 2

    def xs(d):
        return (x + d + N_X) % N_X

    def ys(d):
        return (y + d + N_Y) % N_Y

    def zs(d):
        return (z + d + N_Z) % N_Z

    def at_x(d):
        return _device(xs(d), y, z, c)

    def at_y(d):
        return _device(x, ys(d), z, c)

    def at_z(d):
        return _device(x, y, zs(d), c)

    partner = _device(x, y, z, 1 - c)
    sent = []

    def send(src, dst, device):
        i = len(sent)
        copy = pltpu.make_async_remote_copy(
            src_ref=src, dst_ref=dst, send_sem=ssem.at[i], recv_sem=rsem.at[i],
            device_id=device, device_id_type=MESH,
        )
        copy.start()
        sent.append(copy)
        return copy

    loads = [
        pltpu.make_async_copy(q, qv, lsem.at[0]),
        pltpu.make_async_copy(og, ogv, lsem.at[1]),
        pltpu.make_async_copy(hid, hv.at[pl.ds(0, LEN)], lsem.at[2]),
        pltpu.make_async_copy(k, kv, lsem.at[3]),
        pltpu.make_async_copy(
            w.at[pl.ds(pl.multiple_of(64 * c, 64), 64)], W.at[c, y_lo, z, x], lsem.at[4]
        ),
    ]
    for i, (src, dst) in enumerate(((nlp, nlv), (olp, olv), (rew, rwv), (rlen, rlv), (gid, giv))):
        loads.append(pltpu.make_async_copy(src, dst, lsem.at[5 + i]))
    for i in (5, 6, 7, 8, 9, 4, 3, 0, 1, 2):
        loads[i].start()

    barrier = pltpu.get_barrier_semaphore()
    around = [at_x(1), at_x(-1), at_x(2), at_y(1), at_y(-1), at_y(2), partner]
    around += [at_z(d) for d in range(1, 8)]
    around += [_device(x, ys(2), z, 1 - c)]
    flip = y_hi * 2 + (1 - y_lo)
    around += [_device(xs(d), flip, z, c) for d in range(1, 4)]
    for device in around:
        pl.semaphore_signal(barrier, inc=1, device_id=device, device_id_type=MESH)

    for load in loads[5:]:
        load.wait()
    lane = lax.broadcasted_iota(jnp.int32, (8, 128), 1)
    group = giv[...]
    reward = rwv[...]
    length = rlv[...].astype(F32)
    position = lax.broadcasted_iota(jnp.int32, (1, LEN), 1)
    live = (position < rlv[...]).astype(F32)
    ratio = jnp.exp(nlv[...] - olv[...])
    outside = jnp.logical_or(ratio > 1.28, ratio < 0.8).astype(F32)
    clipped = jnp.sum(live * outside, axis=1, keepdims=True)
    member = (lane % 8 == group).astype(F32)
    stats = jnp.where(
        lane < 8, member,
        jnp.where(
            lane < 16, member * reward,
            jnp.where(
                lane < 24, member * (reward * reward),
                jnp.where(lane == 24, length, jnp.where(lane == 25, clipped, 0.0)),
            ),
        ),
    )
    st[0] = stats
    pl.semaphore_wait(barrier, len(around))

    def stats_steps():
        copies = [send(st.at[0], rsz.at[d - 1], at_z(d)) for d in (4, 3, 5, 2, 6, 1, 7)]
        yield
        for copy in copies:
            copy.wait_recv()
        total = st[0]
        for i in range(7):
            total = total + rsz[i]
        st[1] = total
        plane = [(d, to) for d in (2, 1, 3) for to in (flip, y)] + [(0, flip)]
        copies = [send(st.at[1], rsp.at[i], _device(xs(d), to, z, c)) for i, (d, to) in enumerate(plane)]
        yield
        for copy in copies:
            copy.wait_recv()
        total = st[1]
        for i in range(7):
            total = total + rsp[i]
        st[3] = total
        copies = [
            send(st.at[3], rsc.at[0], at_y(2)),
            send(st.at[3], rsc.at[1], partner),
            send(st.at[3], rsc.at[2], _device(x, ys(2), z, 1 - c)),
        ]
        yield
        for copy in copies:
            copy.wait_recv()
        every = ((st[3] + rsc[0]) + (rsc[1] + rsc[2]))[0:1]
        top = lane[0:1]
        all_live = jnp.sum(jnp.where(top == 24, every, 0.0), axis=1, keepdims=True)
        all_out = jnp.sum(jnp.where(top == 25, every, 0.0), axis=1, keepdims=True)
        cf[...] = all_out / all_live

    def ring_z(view, half):
        up = send(view(z), view(z), at_z(1))
        down = send(view(z), view(z), at_z(-1))
        yield
        for d in (1, 2, 3):
            up.wait_recv()
            down.wait_recv()
            if d < 3:
                up = send(view(zs(-d)), view(zs(-d)), at_z(1))
                down = send(view(zs(d)), view(zs(d)), at_z(-1))
            else:
                up = send(half(zs(-3), 0), half(zs(-3), 0), at_z(1))
                down = send(half(zs(3), 1), half(zs(3), 1), at_z(-1))
            yield
        up.wait_recv()
        down.wait_recv()

    def near_z(view, half):
        copies = [send(view(z), view(z), at_z(d)) for d in (2, -2, 1, -1)]
        yield
        for copy in copies:
            copy.wait_recv()
        below, above = zs(-2), zs(2)
        copies = [
            send(half(below, 0), half(below, 0), at_z(2)),
            send(half(above, 1), half(above, 1), at_z(-2)),
            send(view(below), view(below), at_z(1)),
            send(view(above), view(above), at_z(-1)),
        ]
        yield
        for copy in copies:
            copy.wait_recv()

    forwards = []

    def gather_a():
        own = W.at[c, y_lo, z, x, pl.ds(0, 16)]
        copy = send(own, own, at_y(1))
        yield
        copy.wait_recv()
        yield from near_z(
            lambda i: W.at[c, :, i, x, pl.ds(0, 16)],
            lambda i, h: W.at[c, h, i, x, pl.ds(0, 16)],
        )

        def view(i):
            return W.at[c, :, :, i, pl.ds(0, 16)]

        def half(i, h):
            return W.at[c, h, :, i, pl.ds(0, 16)]

        up = send(view(x), view(x), at_x(1))
        down = send(view(x), view(x), at_x(-1))
        forwards.append(send(view(x), view(x), partner))
        yield
        up.wait_recv()
        down.wait_recv()
        up = send(half(xs(-1), 0), half(xs(-1), 0), at_x(1))
        down = send(half(xs(1), 1), half(xs(1), 1), at_x(-1))
        forwards.append(send(view(xs(-1)), view(xs(-1)), partner))
        forwards.append(send(view(xs(1)), view(xs(1)), partner))
        yield
        up.wait_recv()
        down.wait_recv()
        forwards.append(send(view(xs(2)), view(xs(2)), partner))

    def gather_b():
        own = W.at[c, y_lo, z, x, pl.ds(16, 16)]
        copies = [send(own, own, at_x(d)) for d in (1, 2, 3)]
        yield
        for copy in copies:
            copy.wait_recv()
        left = W.at[c, y_lo, z, pl.ds(0, 2), pl.ds(16, 16)]
        right = W.at[c, y_lo, z, pl.ds(2, 2), pl.ds(16, 16)]
        copies = [send(left, left, at_y(1)), send(right, right, at_y(-1))]
        yield
        for copy in copies:
            copy.wait_recv()
        def view(i):
            return W.at[c, :, i, :, pl.ds(16, 16)]

        yield from ring_z(view, lambda i, h: W.at[c, h, i, :, pl.ds(16, 16)])
        whole = W.at[c, :, :, :, pl.ds(16, 16)]
        forwards.append(send(whole, whole, partner))

    def gather_c():
        yield from near_z(
            lambda i: W.at[c, y_lo, i, x, pl.ds(32, 32)],
            lambda i, h: W.at[c, y_lo, i, x, pl.ds(32 + 16 * h, 16)],
        )
        final = []

        def view(i):
            return W.at[c, y_lo, :, i, pl.ds(32, 32)]

        def half(i, h):
            return W.at[c, y_lo, pl.ds(4 * h, 4), i, pl.ds(32, 32)]

        def across(i):
            final.append(send(half(i, 0), half(i, 0), at_y(1)))
            final.append(send(half(i, 1), half(i, 1), at_y(-1)))

        up = send(view(x), view(x), at_x(1))
        down = send(view(x), view(x), at_x(-1))
        across(x)
        yield
        up.wait_recv()
        down.wait_recv()
        up = send(half(xs(-1), 0), half(xs(-1), 0), at_x(1))
        down = send(half(xs(1), 1), half(xs(1), 1), at_x(-1))
        across(xs(-1))
        across(xs(1))
        yield
        up.wait_recv()
        down.wait_recv()
        across(xs(2))
        mine = W.at[c, y_lo, :, :, pl.ds(32, 32)]
        forwards.append(send(mine, mine, partner))
        yield
        for copy in final:
            copy.wait_recv()
        theirs = W.at[c, 1 - y_lo, :, :, pl.ds(32, 32)]
        forwards.append(send(theirs, theirs, partner))

    done = []

    def advance(steps):
        for step in steps:
            if step not in done and next(step, "end") == "end":
                done.append(step)

    def left(*lists):
        return any(step not in done for steps in lists for step in steps)

    factor = (1.0 / HEAD**0.5) * 1.4426950408889634
    row = lax.broadcasted_iota(jnp.int32, (HEAD, HEAD), 0)
    col = lax.broadcasted_iota(jnp.int32, (HEAD, HEAD), 1)
    causal = row <= col

    def soft(scores):
        top = jnp.max(scores, axis=0, keepdims=True)
        expo = jnp.exp2((scores - top) * factor)
        return (expo * (1.0 / jnp.sum(expo, axis=0, keepdims=True))).astype(BF16)

    def attend(head, first):
        keys = kv[:, head * HEAD:(head + 1) * HEAD]

        def one(i, carry):
            g = first + i
            n = head * GROUP + g
            query = qv[:, pl.ds(pl.multiple_of(n * HEAD, HEAD), HEAD)]
            early = jnp.where(causal, _nt(keys[:128], query[:128]), -1e30)
            late = _nt(keys, query[128:])
            late = jnp.concatenate([late[:128], jnp.where(causal, late[128:], -1e30)], axis=0)
            at = pl.multiple_of(g * LEN, LEN)
            pt[head, pl.ds(0, 128), pl.ds(at, 128)] = soft(early)
            pt[head, pl.ds(128, 128), pl.ds(at, 128)] = jnp.zeros((128, 128), BF16)
            pt[head, :, pl.ds(at + 128, 128)] = soft(late)
            return carry

        lax.fori_loop(0, 4, one, 0)

    attended = []

    def attend_next():
        if not attended:
            loads[3].wait()
            loads[0].wait()
        attend(len(attended) // 2, 4 * (len(attended) % 2))
        attended.append(0)

    def make_coef():
        slice_total = st[3][0:1]
        top = lane[0:1]

        def pick(at):
            return jnp.sum(jnp.where(top == at, slice_total, 0.0), axis=1, keepdims=True)

        own_cnt, own_one, own_two = pick(group), pick(8 + group), pick(16 + group)
        mean = own_one / own_cnt
        var = own_two / own_cnt - mean * mean
        adv = (reward - mean) / jnp.sqrt(var + 0.25)
        total = pick(24) * 4.0
        active = jnp.where(adv > 0, (ratio < 1.28).astype(F32), (ratio > 0.8).astype(F32))
        coef = -live * adv * ratio * active * (65536.0 / total)
        square = (LEN, LEN)
        diagonal = lax.broadcasted_iota(jnp.int32, square, 0) == lax.broadcasted_iota(jnp.int32, square, 1)
        coefv[...] = jnp.broadcast_to(
            jnp.sum(jnp.where(diagonal, coef, 0.0), axis=1, keepdims=True), (LEN, HEAD)
        )
        loads[1].wait()

    def dvalue(core):
        for i in range(2):
            head = 2 * core + i
            for g in range(GROUP):
                columns = pl.ds(pl.multiple_of((head * GROUP + g) * HEAD, HEAD), HEAD)
                douts[g * LEN:(g + 1) * LEN, :] = (coefv[...] * ogv[:, columns].astype(F32)).astype(BF16)
            piece = _nn(pt[head], douts[...]).astype(BF16)
            dvs[core, :, i * HEAD:(i + 1) * HEAD] = piece
            dvf[:, pl.ds(pl.multiple_of(head * HEAD, HEAD), HEAD)] = piece

    dv_copies = []

    def dvalue_other():
        dvalue(1 - c)
        dv_copies.append(send(dvs.at[1 - c], dvr, partner))

    def dvalue_own():
        dvalue(c)
        dvt[:, 0:LEN] = dvs[c].T

    def meet():
        dv_copies[0].wait_recv()
        dvt[:, LEN:2 * LEN] = dvr[...].T
        loads[2].wait()
        hidden_copy.wait_recv()

    def partial(yl, first, count):
        def one(i, carry):
            zz = zs(first + i)
            columns = pl.ds(pl.multiple_of((yl * 8 + zz) * 512, 512), 512)
            block = _nn(dvt[...], hv[:, columns]).astype(BF16)
            for i in range(N_X):
                b = block[:, i * 128:(i + 1) * 128]
                PA[yl, zz, i, 0] = b[0:32]
                PA[yl, zz, i, 1] = b[32:64]
                PB[yl, zz, i, 0] = b[64:96]
                PB[yl, zz, i, 1] = b[96:128]
                PC[yl, zz, i, 0] = b[128:192]
                PC[yl, zz, i, 1] = b[192:256]
            return carry

        lax.fori_loop(0, count, one, 0)

    def added(*terms):
        total = terms[0].astype(F32)
        for term in terms[1:]:
            total = total + term.astype(F32)
        return total

    def reduce_a(first, size):
        part = pl.ds(first, size)
        up = send(PA.at[:, :, xs(2), 0, part], rax.at[0, :, :, part], at_x(1))
        down = send(PA.at[:, :, xs(2), 1, part], rax.at[1, :, :, part], at_x(-1))
        up_b = send(PA.at[:, :, xs(1), 1, part], rax.at[2, :, :, part], at_x(1))
        down_b = send(PA.at[:, :, xs(-1), 0, part], rax.at[3, :, :, part], at_x(-1))
        yield
        up.wait_recv()
        PA[:, :, xs(1), 0, part] = added(PA[:, :, xs(1), 0, part], rax[0, :, :, part]).astype(BF16)
        up = send(PA.at[:, :, xs(1), 0, part], rax.at[4, :, :, part], at_x(1))
        down.wait_recv()
        PA[:, :, xs(-1), 1, part] = added(PA[:, :, xs(-1), 1, part], rax[1, :, :, part]).astype(BF16)
        down = send(PA.at[:, :, xs(-1), 1, part], rax.at[5, :, :, part], at_x(-1))
        yield
        up_b.wait_recv()
        down_b.wait_recv()
        up.wait_recv()
        down.wait_recv()
        PA[:, :, x, 0, part] = added(PA[:, :, x, 0, part], rax[3, :, :, part], rax[4, :, :, part]).astype(BF16)
        PA[:, :, x, 1, part] = added(PA[:, :, x, 1, part], rax[2, :, :, part], rax[5, :, :, part]).astype(BF16)
        copies = [send(PA.at[ys(d) % 2, :, x, ys(d) // 2, part], ray.at[d - 1, :, part], at_y(d)) for d in (2, 1, 3)]
        yield
        for copy in copies:
            copy.wait_recv()
        PA[y_lo, :, x, y_hi, part] = added(PA[y_lo, :, x, y_hi, part], ray[0, :, part], ray[1, :, part], ray[2, :, part]).astype(BF16)
        copies = [send(PA.at[y_lo, zs(d), x, y_hi, part], raz.at[d - 1, part], at_z(d)) for d in (4, 3, 5, 2, 6, 1, 7)]
        yield
        for copy in copies:
            copy.wait_recv()
        fin[y_hi, c, part] = added(PA[y_lo, z, x, y_hi, part], *[raz[i, part] for i in range(7)]).astype(BF16)

    def reduce_c(first, size):
        part = pl.ds(first, size)

        def view(d, h):
            return PC.at[ys(d) % 2, pl.ds(4 * h, 4), :, ys(d) // 2, part]

        def get(d, h):
            return PC[ys(d) % 2, pl.ds(4 * h, 4), :, ys(d) // 2, part]

        def put(d, h, value):
            PC[ys(d) % 2, pl.ds(4 * h, 4), :, ys(d) // 2, part] = value.astype(BF16)

        up = send(view(2, 0), rcy.at[0, :, :, part], at_y(1))
        down = send(view(2, 1), rcy.at[1, :, :, part], at_y(-1))
        yield
        up_b = send(view(1, 1), rcy.at[2, :, :, part], at_y(1))
        down_b = send(view(-1, 0), rcy.at[3, :, :, part], at_y(-1))
        yield
        up.wait_recv()
        put(1, 0, added(get(1, 0), rcy[0, :, :, part]))
        up = send(view(1, 0), rcy.at[4, :, :, part], at_y(1))
        down.wait_recv()
        put(-1, 1, added(get(-1, 1), rcy[1, :, :, part]))
        down = send(view(-1, 1), rcy.at[5, :, :, part], at_y(-1))
        yield
        up_b.wait_recv()
        down_b.wait_recv()
        up.wait_recv()
        down.wait_recv()
        put(0, 0, added(get(0, 0), rcy[3, :, :, part], rcy[4, :, :, part]))
        put(0, 1, added(get(0, 1), rcy[2, :, :, part], rcy[5, :, :, part]))
        copies = [send(PC.at[y_lo, :, xs(d), y_hi, part], rcx.at[d - 1, :, part], at_x(d)) for d in (2, 1, 3)]
        yield
        for copy in copies:
            copy.wait_recv()
        PC[y_lo, :, x, y_hi, part] = added(PC[y_lo, :, x, y_hi, part], rcx[0, :, part], rcx[1, :, part], rcx[2, :, part]).astype(BF16)
        copies = [send(PC.at[y_lo, zs(d), x, y_hi, part], rcz.at[d - 1, part], at_z(d)) for d in (4, 3, 5, 2, 6, 1, 7)]
        yield
        for copy in copies:
            copy.wait_recv()
        fin[y_hi, c, pl.ds(RA + RB + first, size)] = added(
            PC[y_lo, z, x, y_hi, part], *[rcz[i, part] for i in range(7)]
        ).astype(BF16)

    def reduce_b(first, size):
        part = pl.ds(first, size)
        up = send(PB.at[:, zs(4), :, 0, part], rbz.at[0, :, :, 0, part], at_z(1))
        down = send(PB.at[:, zs(4), :, 1, part], rbz.at[0, :, :, 1, part], at_z(-1))
        yield
        up.wait_recv()
        PB[:, zs(3), :, 0, part] = added(PB[:, zs(3), :, 0, part], rbz[0, :, :, 0, part]).astype(BF16)
        up = send(PB.at[:, zs(3), :, :, part], rbz.at[1, :, :, :, part], at_z(1))
        down.wait_recv()
        PB[:, zs(-3), :, 1, part] = added(PB[:, zs(-3), :, 1, part], rbz[0, :, :, 1, part]).astype(BF16)
        down = send(PB.at[:, zs(-3), :, :, part], rbz.at[2, :, :, :, part], at_z(-1))
        yield
        for d in (2, 1):
            up.wait_recv()
            PB[:, zs(d), :, :, part] = added(PB[:, zs(d), :, :, part], rbz[5 - 2 * d, :, :, :, part]).astype(BF16)
            up = send(PB.at[:, zs(d), :, :, part], rbz.at[7 - 2 * d, :, :, :, part], at_z(1))
            down.wait_recv()
            PB[:, zs(-d), :, :, part] = added(PB[:, zs(-d), :, :, part], rbz[6 - 2 * d, :, :, :, part]).astype(BF16)
            down = send(PB.at[:, zs(-d), :, :, part], rbz.at[8 - 2 * d, :, :, :, part], at_z(-1))
            yield
        up.wait_recv()
        down.wait_recv()
        PB[:, z, :, :, part] = added(PB[:, z, :, :, part], rbz[5, :, :, :, part], rbz[6, :, :, :, part]).astype(BF16)
        copies = [send(PB.at[:, z, xs(d), :, part], rbx.at[d - 1, :, :, part], at_x(d)) for d in (2, 1, 3)]
        yield
        for copy in copies:
            copy.wait_recv()
        PB[:, z, x, :, part] = added(PB[:, z, x, :, part], rbx[0, :, :, part], rbx[1, :, :, part], rbx[2, :, :, part]).astype(BF16)
        copies = [send(PB.at[ys(d) % 2, z, x, ys(d) // 2, part], rby.at[d - 1, part], at_y(d)) for d in (2, 1, 3)]
        yield
        for copy in copies:
            copy.wait_recv()
        fin[y_hi, c, pl.ds(RA + first, size)] = added(PB[y_lo, z, x, y_hi, part], rby[0, part], rby[1, part], rby[2, part]).astype(BF16)

    def product(t, carry):
        yl, zz = t // 8, t % 8
        rows = jnp.concatenate([W[h, yl, zz, i] for i in range(N_X) for h in range(2)], axis=0)
        ig[:, pl.ds(pl.multiple_of(t * 512, 512), 512)] = _nt(dvf[...], rows).astype(BF16)
        return carry

    products = []

    def product_next():
        if not products:
            for copy in forwards:
                copy.wait_recv()
        first = 2 * len(products)
        lax.fori_loop(first, first + 2, product, 0)
        products.append(0)

    steps = {
        "stat": stats_steps(),
        "ga": gather_a(),
        "gb": gather_b(),
        "gc": gather_c(),
        "ra": reduce_a(0, RA),
        "rb": reduce_b(0, RB),
        "rc": reduce_c(0, 32),
        "rd": reduce_c(32, 32),
    }

    def partial_first():
        meet()
        partial(y_lo, 4, 1)
        partial(1 - y_lo, 4, 1)

    def partial_third():
        partial(1 - y_lo, 3, 1)
        partial(1 - y_lo, 5, 1)

    work = {
        "att": attend_next,
        "coef": make_coef,
        "pass2a": dvalue_other,
        "pass2b": dvalue_own,
        "part0": partial_first,
        "part1": lambda: partial(y_lo, 5, 7),
        "part2": partial_third,
        "part3": lambda: partial(1 - y_lo, 6, 5),
        "prod": product_next,
    }
    hidden_copy = send(hid, hv.at[pl.ds(LEN, LEN)], partner)
    loads[4].wait()
    for name in ORDER:
        if name in work:
            work[name]()
        else:
            advance([steps[name]])
    advance(list(steps.values()))
    while left(steps.values()):
        advance(list(steps.values()))

    mine = fin.at[y_hi, c]
    copies = [
        send(mine, mine, at_y(2)),
        send(mine, mine, partner),
        send(mine, mine, _device(x, ys(2), z, 1 - c)),
    ]
    for copy in copies:
        copy.wait_recv()
    pieces = []
    for core in range(2):
        for first, size in ((0, RA), (RA, RB), (RA + RB, RC)):
            for half in range(2):
                pieces.append(fin[half, core, pl.ds(first, size)])
    wg[...] = jnp.concatenate(pieces, axis=0).astype(F32).T

    for copy in sent:
        copy.wait_send()


def write_out(ig, wg, ig_out, wg_out, sem):
    rows = LEN // 8
    copies = [pltpu.make_async_copy(wg, wg_out, sem.at[8])]
    for i in range(8):
        part = pl.ds(i * rows, rows)
        copies.append(pltpu.make_async_copy(ig.at[part], ig_out.at[part], sem.at[i]))
    for copy in copies:
        copy.start()
    for copy in copies:
        copy.wait()


def local(
    hidden_in, value_weight, queries, keys, out_grad, new_logp, old_logp, rewards, resp_len, group_id
):
    vmem = pl.BlockSpec(memory_space=pltpu.VMEM)
    hbm = pl.BlockSpec(memory_space=pltpu.HBM)
    bf = functools.partial(pltpu.VMEM, dtype=BF16)
    scratch = [
        bf((2 * LEN, D)),
        bf((LEN, 4096)),
        bf((LEN, 4096)),
        bf((LEN, 512)),
        bf((KV_HEADS, LEN, GROUP * LEN)),
        bf((GROUP * LEN, HEAD)),
        bf((2, LEN, 256)),
        bf((LEN, 512)),
        bf((LEN, 256)),
        bf((256, 2 * LEN)),
        bf((2, 2, 8, 4, 64, 512)),
        bf((2, 8, 4, 2, RA, 128)),
        bf((2, 8, 4, 2, RB, 128)),
        bf((2, 8, 4, 2, RC, 128)),
        bf((6, 2, 8, RA, 128)),
        bf((3, 8, RA, 128)),
        bf((7, RA, 128)),
        bf((6, 4, 4, RC, 128)),
        bf((3, 8, RC, 128)),
        bf((7, RC, 128)),
        bf((7, 2, 4, 2, RB, 128)),
        bf((3, 2, 2, RB, 128)),
        bf((3, RB, 128)),
        bf((2, 2, 128, 128)),
        pltpu.VMEM((4, 8, 128), F32),
        pltpu.VMEM((7, 8, 128), F32),
        pltpu.VMEM((7, 8, 128), F32),
        pltpu.VMEM((3, 8, 128), F32),
        pltpu.VMEM((LEN, HEAD), F32),
        pltpu.SemaphoreType.DMA((SLOTS,)),
        pltpu.SemaphoreType.DMA((SLOTS,)),
        pltpu.SemaphoreType.DMA((10,)),
        pltpu.VMEM((1, LEN), F32),
        pltpu.VMEM((1, LEN), F32),
        pltpu.VMEM((1, 1), F32),
        pltpu.VMEM((1, 1), jnp.int32),
        pltpu.VMEM((1, 1), jnp.int32),
    ]
    input_grad, weight_grad, clip_frac = pl.pallas_call(
        kernel,
        out_shape=(
            pltpu.VMEM((LEN, D), BF16),
            pltpu.VMEM((128, 512), F32),
            jax.ShapeDtypeStruct((1, 1), F32),
        ),
        in_specs=[hbm] * 10,
        out_specs=(vmem, vmem, vmem),
        scratch_shapes=scratch,
        compiler_params=pltpu.CompilerParams(
            collective_id=0, has_side_effects=True, vmem_limit_bytes=56 << 20
        ),
        name="value_backward",
    )(
        hidden_in, value_weight, queries, keys, out_grad,
        new_logp.reshape(1, LEN), old_logp.reshape(1, LEN), rewards.reshape(1, 1), resp_len, group_id,
    )
    input_grad, weight_grad = pl.pallas_call(
        write_out,
        out_shape=(
            jax.ShapeDtypeStruct((LEN, D), BF16),
            jax.ShapeDtypeStruct((128, 512), F32),
        ),
        in_specs=[vmem, vmem],
        out_specs=(hbm, hbm),
        scratch_shapes=[pltpu.SemaphoreType.DMA((9,))],
        compiler_params=pltpu.CompilerParams(vmem_limit_bytes=4 << 20),
        name="write_out",
    )(input_grad, weight_grad)
    return input_grad, weight_grad, clip_frac.reshape(())


def solution(mesh):
    rows = P(("cuts", "fsdp"), None)
    flat = P(("cuts", "fsdp"))
    return jax.shard_map(
        local,
        mesh=mesh,
        in_specs=(
            rows, P("fsdp", None), rows, rows, rows, flat, flat, flat, P("cuts", "fsdp"), P("cuts", "fsdp"),
        ),
        out_specs=(rows, P("fsdp", None), P()),
        check_vma=False,
    )
```

time: 115 us -> 80.7 us (0.70)
  Pallas kernels: 105 us -> 76.2 us
  local copies, waits for them, and re-layouts: 5.39 us -> 0 us
    pallas_call x1 -> x2, Pallas kernels: 105 us -> 76.2 us  [the longest x1 74.1 us: local(): pl.pallas_call(kernel, out_shape=(pltpu.VMEM((LEN, D), BF16), pltpu.VMEM(...]
    unnamed x4 -> x0, local copies, waits for them, and re-layouts: 5.39 us -> none
where the time goes in v2:
time: 80.7 us; the launch traced here: 80.6 us
  Pallas kernels  76.2 us (94%)
  between operations  4.34 us (5%)
    pallas_call x1, Pallas kernels, local(): pl.pallas_call(kernel, out_shape=(pltpu.VMEM((LEN, D), BF16), pltpu.VMEM(...  74.1 us
    pallas_call x1, Pallas kernels, local(): pl.pallas_call(write_out, out_shape=(jax.ShapeDtypeStruct((LEN, D), BF16)...  2.17 us

profile of v2, /device:TPU:1, one launch (start us, length us, event | category | flops | bytes accessed | tf_op | source)
XLA Modules:
  0.0 80.6 jit_solution(14640291718253649549)
XLA Ops:
  2.6 74.1 %value_backward.1 = (bf16[256,8192]{1,0:T(8,128)(2,1)S(1)}, f32[128,512]{1,0:T(8,128)S(1)}, f32[1,1]{1,0:T(1,128)}) custom-call(bf16[256,8192]{1,0:T(8,128)(2,1)} %hid.1, bf16[128,512]{1,0:T(8,128)(2,1)} %w.1, bf16[256,4096]{1,0:T(8,128)(2,1)} %q.1, bf16[256,512]{1,0:T(8,128)(2,1)} %k.1, bf16[256,4096]{1,0:T(8,128)(2,1)} %og.1, f32[1,256]{1,0:T(1,128)} %bitcast.5, ...), custom_call_target="tpu_custom_call" | custom-call | tf_op jit(solution)/shard_map/value_backward/pallas_call | solution.py:662
  76.7 2.2 %write_out.1 = (bf16[256,8192]{1,0:T(8,128)(2,1)}, f32[128,512]{1,0:T(8,128)}) custom-call(bf16[256,8192]{1,0:T(8,128)(2,1)S(1)} %get-tuple-element.8.ig, f32[128,512]{1,0:T(8,128)S(1)} %get-tuple-element.9.wg), custom_call_target="tpu_custom_call" | custom-call | tf_op jit(solution)/shard_map/write_out/pallas_call | solution.py:680

commit v3 on v2

--- a/solution.py
+++ b/solution.py
@@ -23,10 +23,10 @@
     "att", "gb", "att", "stat", "gc", "att", "gb", "ga", "gc", "stat",
     "coef", "pass2a", "pass2b", "part0", "rb", "gb", "part1", "rc", "ga", "part2",
     "part3", "ra", "gc", "rc", "rb", "rd", "rd", "gb", "rc", "rb",
-    "ga", "gb", "ra", "rb", "gb", "rd", "gc", "gb", "rb", "ga",
-    "ga", "rc", "ra", "rb", "rd", "rc", "gc", "rd", "ra", "gc",
-    "prod", "rb", "rc", "prod", "prod", "prod", "prod", "rd", "prod", "prod",
-    "ra", "prod",
+    "ga", "gb", "ra", "rb", "gb", "rd", "gc", "gc", "gc", "rb",
+    "ga", "prod", "prod", "prod", "ra", "rc", "prod", "rb", "prod", "rd",
+    "prod", "gc", "rc", "prod", "prod", "ra", "rd", "rb", "rc", "ra",
+    "rd",
 )
 
 
@@ -173,7 +173,7 @@
         top = lane[0:1]
         all_live = jnp.sum(jnp.where(top == 24, every, 0.0), axis=1, keepdims=True)
         all_out = jnp.sum(jnp.where(top == 25, every, 0.0), axis=1, keepdims=True)
-        cf[...] = all_out / all_live
+        cf[...] = jnp.broadcast_to(all_out / all_live, (1, 128))
 
     def ring_z(view, half):
         up = send(view(z), view(z), at_z(1))
@@ -208,7 +208,10 @@
         for copy in copies:
             copy.wait_recv()
 
-    forwards = []
+    forwards = {}
+
+    def forward(key, ref):
+        forwards.setdefault(key, []).append(send(ref, ref, partner))
 
     def gather_a():
         own = W.at[c, y_lo, z, x, pl.ds(0, 16)]
@@ -228,18 +231,18 @@
 
         up = send(view(x), view(x), at_x(1))
         down = send(view(x), view(x), at_x(-1))
-        forwards.append(send(view(x), view(x), partner))
+        forward("A0", view(x))
         yield
         up.wait_recv()
         down.wait_recv()
         up = send(half(xs(-1), 0), half(xs(-1), 0), at_x(1))
         down = send(half(xs(1), 1), half(xs(1), 1), at_x(-1))
-        forwards.append(send(view(xs(-1)), view(xs(-1)), partner))
-        forwards.append(send(view(xs(1)), view(xs(1)), partner))
-        yield
-        up.wait_recv()
-        down.wait_recv()
-        forwards.append(send(view(xs(2)), view(xs(2)), partner))
+        forward("A1", view(xs(-1)))
+        forward("A1", view(xs(1)))
+        yield
+        up.wait_recv()
+        down.wait_recv()
+        forward("A2", view(xs(2)))
 
     def gather_b():
         own = W.at[c, y_lo, z, x, pl.ds(16, 16)]
@@ -258,7 +261,7 @@
 
         yield from ring_z(view, lambda i, h: W.at[c, h, i, :, pl.ds(16, 16)])
         whole = W.at[c, :, :, :, pl.ds(16, 16)]
-        forwards.append(send(whole, whole, partner))
+        forward("B", whole)
 
     def gather_c():
         yield from near_z(
@@ -291,13 +294,18 @@
         up.wait_recv()
         down.wait_recv()
         across(xs(2))
-        mine = W.at[c, y_lo, :, :, pl.ds(32, 32)]
-        forwards.append(send(mine, mine, partner))
-        yield
-        for copy in final:
-            copy.wait_recv()
-        theirs = W.at[c, 1 - y_lo, :, :, pl.ds(32, 32)]
-        forwards.append(send(theirs, theirs, partner))
+        forward("M", W.at[c, y_lo, :, :, pl.ds(32, 32)])
+        yield
+        for key, copies, places in (
+            ("C0", final[0:2], (x,)),
+            ("C1", final[2:6], (xs(-1), xs(1))),
+            ("C2", final[6:8], (xs(2),)),
+        ):
+            for copy in copies:
+                copy.wait_recv()
+            for i in places:
+                forward(key, W.at[c, 1 - y_lo, :, i, pl.ds(32, 32)])
+            yield
 
     done = []
 
@@ -335,7 +343,7 @@
             pt[head, :, pl.ds(at + 128, 128)] = soft(late)
             return carry
 
-        lax.fori_loop(0, 4, one, 0)
+        lax.fori_loop(0, 4, one, 0, unroll=2)
 
     attended = []
 
@@ -408,7 +416,7 @@
                 PC[yl, zz, i, 1] = b[192:256]
             return carry
 
-        lax.fori_loop(0, count, one, 0)
+        lax.fori_loop(0, count, one, 0, unroll=True)
 
     def added(*terms):
         total = terms[0].astype(F32)
@@ -525,20 +533,29 @@
             copy.wait_recv()
         fin[y_hi, c, pl.ds(RA + first, size)] = added(PB[y_lo, z, x, y_hi, part], rby[0, part], rby[1, part], rby[2, part]).astype(BF16)
 
-    def product(t, carry):
-        yl, zz = t // 8, t % 8
-        rows = jnp.concatenate([W[h, yl, zz, i] for i in range(N_X) for h in range(2)], axis=0)
-        ig[:, pl.ds(pl.multiple_of(t * 512, 512), 512)] = _nt(dvf[...], rows).astype(BF16)
-        return carry
+    def product(yl, i):
+        def one(t, carry):
+            first = 4 * t
+            rows = [W[h, yl, first + j, i] for j in range(4) for h in range(2)]
+            block = _nt(dvf[...], jnp.concatenate(rows, axis=0)).astype(BF16)
+            for j in range(4):
+                at = ((yl * 8 + first + j) * 4 + i) * 128
+                ig[:, pl.ds(pl.multiple_of(at, 128), 128)] = block[:, j * 128:(j + 1) * 128]
+            return carry
+
+        lax.fori_loop(0, 2, one, 0, unroll=True)
 
     products = []
 
     def product_next():
-        if not products:
-            for copy in forwards:
-                copy.wait_recv()
-        first = 2 * len(products)
-        lax.fori_loop(first, first + 2, product, 0)
+        n = len(products)
+        place = n // 2
+        group = (0, 1, 1, 2)[place]
+        if n in (0, 2, 6):
+            for key in ("B", "M", "A0", "C0") if n == 0 else ("A%d" % group, "C%d" % group):
+                for copy in forwards[key]:
+                    copy.wait_recv()
+        product(n % 2, (x, xs(-1), xs(1), xs(2))[place])
         products.append(0)
 
     steps = {
@@ -602,9 +619,9 @@
         copy.wait_send()
 
 
-def write_out(ig, wg, ig_out, wg_out, sem):
+def write_out(ig, wg, cf, ig_out, wg_out, cf_out, sem):
     rows = LEN // 8
-    copies = [pltpu.make_async_copy(wg, wg_out, sem.at[8])]
+    copies = [pltpu.make_async_copy(wg, wg_out, sem.at[8]), pltpu.make_async_copy(cf, cf_out, sem.at[9])]
     for i in range(8):
         part = pl.ds(i * rows, rows)
         copies.append(pltpu.make_async_copy(ig.at[part], ig_out.at[part], sem.at[i]))
@@ -664,7 +681,7 @@
         out_shape=(
             pltpu.VMEM((LEN, D), BF16),
             pltpu.VMEM((128, 512), F32),
-            jax.ShapeDtypeStruct((1, 1), F32),
+            pltpu.VMEM((1, 128), F32),
         ),
         in_specs=[hbm] * 10,
         out_specs=(vmem, vmem, vmem),
@@ -677,19 +694,20 @@
         hidden_in, value_weight, queries, keys, out_grad,
         new_logp.reshape(1, LEN), old_logp.reshape(1, LEN), rewards.reshape(1, 1), resp_len, group_id,
     )
-    input_grad, weight_grad = pl.pallas_call(
+    input_grad, weight_grad, clip_frac = pl.pallas_call(
         write_out,
         out_shape=(
             jax.ShapeDtypeStruct((LEN, D), BF16),
             jax.ShapeDtypeStruct((128, 512), F32),
+            jax.ShapeDtypeStruct((1, 128), F32),
         ),
-        in_specs=[vmem, vmem],
-        out_specs=(hbm, hbm),
-        scratch_shapes=[pltpu.SemaphoreType.DMA((9,))],
+        in_specs=[vmem, vmem, vmem],
+        out_specs=(hbm, hbm, hbm),
+        scratch_shapes=[pltpu.SemaphoreType.DMA((10,))],
         compiler_params=pltpu.CompilerParams(vmem_limit_bytes=4 << 20),
         name="write_out",
-    )(input_grad, weight_grad)
-    return input_grad, weight_grad, clip_frac.reshape(())
+    )(input_grad, weight_grad, clip_frac)
+    return input_grad, weight_grad, clip_frac[0, 0]
 
 
 def solution(mesh):

time: 80.7 us -> 73.7 us (0.913)
  Pallas kernels: 76.2 us -> 71 us
  between operations: 4.34 us -> 2.58 us
    pallas_call x1, Pallas kernels: 74.1 us -> 68.8 us  [local(): pl.pallas_call(kernel, out_shape=(pltpu.VMEM((LEN, D), BF16), pltpu.VMEM(...]
where the time goes in v3:
time: 73.7 us; the launch traced here: 73.6 us
  Pallas kernels  71 us (96%)
  between operations  2.58 us (4%)
    pallas_call x1, Pallas kernels, local(): pl.pallas_call(kernel, out_shape=(pltpu.VMEM((LEN, D), BF16), pltpu.VMEM(...  68.8 us
    pallas_call x1, Pallas kernels, local(): pl.pallas_call(write_out, out_shape=(jax.ShapeDtypeStruct((LEN, D), BF16)...  2.18 us

profile of v3, /device:TPU:1, one launch (start us, length us, event | category | flops | bytes accessed | tf_op | source)
XLA Modules:
  0.0 73.6 jit_solution(2119592537969021158)
XLA Ops:
  2.6 68.8 %value_backward.1 = (bf16[256,8192]{1,0:T(8,128)(2,1)S(1)}, f32[128,512]{1,0:T(8,128)S(1)}, f32[1,128]{1,0:T(1,128)S(1)}) custom-call(bf16[256,8192]{1,0:T(8,128)(2,1)} %hid.1, bf16[128,512]{1,0:T(8,128)(2,1)} %w.1, bf16[256,4096]{1,0:T(8,128)(2,1)} %q.1, bf16[256,512]{1,0:T(8,128)(2,1)} %k.1, bf16[256,4096]{1,0:T(8,128)(2,1)} %og.1, f32[1,256]{1,0:T(1,128)} %bitcast.6, ...), custom_call_target="tpu_custom_call" | custom-call | tf_op jit(solution)/shard_map/value_backward/pallas_call | solution.py:679
  71.4 2.2 %write_out.1 = (bf16[256,8192]{1,0:T(8,128)(2,1)}, f32[128,512]{1,0:T(8,128)}, f32[1,128]{1,0:T(1,128)}) custom-call(bf16[256,8192]{1,0:T(8,128)(2,1)S(1)} %get-tuple-element.9.ig, f32[128,512]{1,0:T(8,128)S(1)} %get-tuple-element.10.wg, f32[1,128]{1,0:T(1,128)S(1)} %get-tuple-element.11.cf), custom_call_target="tpu_custom_call" | custom-call | tf_op jit(solution)/shard_map/write_out/pallas_call | solution.py:697

commit v4 on v3

--- a/solution.py
+++ b/solution.py
@@ -24,9 +24,9 @@
     "coef", "pass2a", "pass2b", "part0", "rb", "gb", "part1", "rc", "ga", "part2",
     "part3", "ra", "gc", "rc", "rb", "rd", "rd", "gb", "rc", "rb",
     "ga", "gb", "ra", "rb", "gb", "rd", "gc", "gc", "gc", "rb",
-    "ga", "prod", "prod", "prod", "ra", "rc", "prod", "rb", "prod", "rd",
-    "prod", "gc", "rc", "prod", "prod", "ra", "rd", "rb", "rc", "ra",
-    "rd",
+    "ga", "ra", "prod", "rc", "prod", "prod", "rb", "prod", "prod", "rd",
+    "prod", "prod", "gc", "rc", "prod", "prod", "ra", "prod", "prod", "rd",
+    "prod", "prod", "rb", "prod", "prod", "rc", "ra", "prod", "rd",
 )
 
 
@@ -533,29 +533,24 @@
             copy.wait_recv()
         fin[y_hi, c, pl.ds(RA + first, size)] = added(PB[y_lo, z, x, y_hi, part], rby[0, part], rby[1, part], rby[2, part]).astype(BF16)
 
-    def product(yl, i):
-        def one(t, carry):
-            first = 4 * t
-            rows = [W[h, yl, first + j, i] for j in range(4) for h in range(2)]
-            block = _nt(dvf[...], jnp.concatenate(rows, axis=0)).astype(BF16)
-            for j in range(4):
-                at = ((yl * 8 + first + j) * 4 + i) * 128
-                ig[:, pl.ds(pl.multiple_of(at, 128), 128)] = block[:, j * 128:(j + 1) * 128]
-            return carry
-
-        lax.fori_loop(0, 2, one, 0, unroll=True)
+    def product(yl, first, i):
+        rows = [W[h, yl, first + j, i] for j in range(4) for h in range(2)]
+        block = _nt(dvf[...], jnp.concatenate(rows, axis=0)).astype(BF16)
+        for j in range(4):
+            at = ((yl * 8 + first + j) * 4 + i) * 128
+            ig[:, pl.ds(pl.multiple_of(at, 128), 128)] = block[:, j * 128:(j + 1) * 128]
 
     products = []
 
     def product_next():
         n = len(products)
-        place = n // 2
+        place = n // 4
         group = (0, 1, 1, 2)[place]
-        if n in (0, 2, 6):
+        if n in (0, 4, 12):
             for key in ("B", "M", "A0", "C0") if n == 0 else ("A%d" % group, "C%d" % group):
                 for copy in forwards[key]:
                     copy.wait_recv()
-        product(n % 2, (x, xs(-1), xs(1), xs(2))[place])
+        product(n // 2 % 2, 4 * (n % 2), (x, xs(-1), xs(1), xs(2))[place])
         products.append(0)
 
     steps = {

time: 73.7 us -> 73.3 us (level)
  no operation moved by 1% of the time
where the time goes in v4:
time: 73.3 us; the launch traced here: 73.2 us
  Pallas kernels  70.6 us (96%)
  between operations  2.58 us (4%)
    pallas_call x1, Pallas kernels, local(): pl.pallas_call(kernel, out_shape=(pltpu.VMEM((LEN, D), BF16), pltpu.VMEM(...  68.4 us
    pallas_call x1, Pallas kernels, local(): pl.pallas_call(write_out, out_shape=(jax.ShapeDtypeStruct((LEN, D), BF16)...  2.18 us

profile of v4, /device:TPU:1, one launch (start us, length us, event | category | flops | bytes accessed | tf_op | source)
XLA Modules:
  0.0 73.2 jit_solution(1211565781594921274)
XLA Ops:
  2.6 68.4 %value_backward.1 = (bf16[256,8192]{1,0:T(8,128)(2,1)S(1)}, f32[128,512]{1,0:T(8,128)S(1)}, f32[1,128]{1,0:T(1,128)S(1)}) custom-call(bf16[256,8192]{1,0:T(8,128)(2,1)} %hid.1, bf16[128,512]{1,0:T(8,128)(2,1)} %w.1, bf16[256,4096]{1,0:T(8,128)(2,1)} %q.1, bf16[256,512]{1,0:T(8,128)(2,1)} %k.1, bf16[256,4096]{1,0:T(8,128)(2,1)} %og.1, f32[1,256]{1,0:T(1,128)} %bitcast.6, ...), custom_call_target="tpu_custom_call" | custom-call | tf_op jit(solution)/shard_map/value_backward/pallas_call | solution.py:674
  71.0 2.2 %write_out.1 = (bf16[256,8192]{1,0:T(8,128)(2,1)}, f32[128,512]{1,0:T(8,128)}, f32[1,128]{1,0:T(1,128)}) custom-call(bf16[256,8192]{1,0:T(8,128)(2,1)S(1)} %get-tuple-element.9.ig, f32[128,512]{1,0:T(8,128)S(1)} %get-tuple-element.10.wg, f32[1,128]{1,0:T(1,128)S(1)} %get-tuple-element.11.cf), custom_call_target="tpu_custom_call" | custom-call | tf_op jit(solution)/shard_map/write_out/pallas_call | solution.py:692
